TPU v7x, 32 devices: a whole 2x2x4 slice. The times are simulated.
32 devices in a mesh: gz: 8 (over z, x), gx: 4 (over y, core).
Axes of the slice: x: 2, y: 2, z: 4, core: 2. Of those that a mesh axis runs over, the one named last changes fastest.
Arguments:
- d_field: float32 [3, 64, 128, 128], P(None, 'gz', 'gx'), may hold values from -6 to 6
- e_field: float32 [3, 64, 128, 128], P(None, 'gz', 'gx'), may hold values from -6 to 6
- h_field: float32 [3, 64, 128, 128], P(None, 'gz', 'gx'), may hold values from -6 to 6
- permittivity: float32 [64, 128, 128], P('gz', 'gx'), may hold values from 1 to 4
- kerr_coeff: float32 [64, 128, 128], P('gz', 'gx'), may hold values from 0.05 to 0.3
- classes: int32 [2, 128, 128], P(None, 'gx'), may hold values from 0 to 7
- eps_table: float32 [8], replicated, may hold values from 1 to 6
- chi_table: float32 [8], replicated, may hold values from 0.02 to 0.4
Outputs:
- d_out: float32 [3, 64, 128, 128], P(None, 'gz', 'gx')
- e_out: float32 [3, 64, 128, 128], P(None, 'gz', 'gx')
- h_out: float32 [3, 64, 128, 128], P(None, 'gz', 'gx')
- eps_out: float32 [64, 128, 128], P('gz', 'gx')
- chi_out: float32 [64, 128, 128], P('gz', 'gx')
All inputs are finite; a program needn't handle non-finite values.
Results may differ from a plain program's by a relative error of at most 0.00002.
Values sent between devices are 32-bit elements; how exact they have to be, the bound alone decides.
A program may use at most 64 MiB of HBM per device.

v0:
```python
import jax
import jax.numpy as jnp
from jax import lax
from jax.sharding import PartitionSpec as P

STEPS = 4
KERR = 3
ADVANCE = 2


courant = 0.5


def with_halo(cells, sides, width):
    for axis, dim in sides:
        count = lax.axis_size(axis)
        ends = count - 1
        head = lax.slice_in_dim(cells, 0, width, axis=dim)
        tail = lax.slice_in_dim(cells, cells.shape[dim] - width, cells.shape[dim], axis=dim)
        cells = jnp.concatenate(
            [
                lax.ppermute(tail, axis, [(i, (i + 1) % count) for i in range(ends)]),
                cells,
                lax.ppermute(head, axis, [((i + 1) % count, i) for i in range(ends)]),
            ],
            axis=dim,
        )
    return cells


def ahead_any(values, along):
    size = values.shape[along]
    tail = lax.slice_in_dim(values, 1, size, axis=along)
    zeros = jnp.zeros_like(lax.slice_in_dim(values, 0, 1, axis=along))
    return jnp.concatenate([tail, zeros], axis=along)


def behind_any(values, along):
    size = values.shape[along]
    head = lax.slice_in_dim(values, 0, size - 1, axis=along)
    zeros = jnp.zeros_like(lax.slice_in_dim(values, 0, 1, axis=along))
    return jnp.concatenate([zeros, head], axis=along)


def local_curl_ahead(field):
    curl_x = ahead_any(field[2], 2) - field[2] - (ahead_any(field[1], 0) - field[1])
    curl_y = ahead_any(field[0], 0) - field[0] - (ahead_any(field[2], 1) - field[2])
    curl_z = ahead_any(field[1], 1) - field[1] - (ahead_any(field[0], 2) - field[0])
    return jnp.stack([curl_x, curl_y, curl_z])


def local_curl_behind(field):
    curl_x = field[2] - behind_any(field[2], 2) - (field[1] - behind_any(field[1], 0))
    curl_y = field[0] - behind_any(field[0], 0) - (field[2] - behind_any(field[2], 1))
    curl_z = field[1] - behind_any(field[1], 1) - (field[0] - behind_any(field[0], 2))
    return jnp.stack([curl_x, curl_y, curl_z])


def lookup(classes, table):
    labels = jnp.arange(table.shape[0], dtype=jnp.int32).reshape(-1, 1, 1, 1)
    picked = jnp.where(classes[None] == labels, table.reshape(-1, 1, 1, 1), jnp.float32(0.0))
    return jnp.sum(picked, axis=0)


def on_device(d_field, e_field, h_field, permittivity, kerr_coeff, classes, eps_table, chi_table):
    is_last = lax.axis_index("gz") == lax.axis_size("gz") - 1
    planes_dev = d_field.shape[1]
    rows_dev = d_field.shape[2]
    reach = STEPS + ADVANCE
    block = jnp.concatenate(
        [d_field, e_field, h_field, permittivity[None], kerr_coeff[None]], axis=0
    )
    deeper = with_halo(block, (("gz", 1),), reach)
    padded = with_halo(deeper, (("gx", 2),), STEPS)
    plane_ids = (
        lax.axis_index("gz") * planes_dev - reach + jnp.arange(padded.shape[1], dtype=jnp.int32)
    )
    row_ids = lax.axis_index("gx") * rows_dev - STEPS + jnp.arange(padded.shape[2], dtype=jnp.int32)
    plane_in = (plane_ids >= 0) & (plane_ids < planes_dev * lax.axis_size("gz"))
    row_in = (row_ids >= 0) & (row_ids < rows_dev * lax.axis_size("gx"))
    inside = plane_in[:, None, None] & row_in[None, :, None]
    weight = inside.astype(jnp.float32)
    displace, electric, magnetic = (padded[0:3], padded[3:6], padded[6:9])
    perm_local = jnp.where(inside, padded[9], jnp.float32(1.0))
    chi_local = padded[10] * weight
    for sweep in range(STEPS):
        magnetic = (magnetic - courant * local_curl_ahead(electric)) * weight[None]
        displace = (displace + courant * local_curl_behind(magnetic)) * weight[None]
        for inner in range(KERR):
            energy = (
                electric[0] * electric[0] + electric[1] * electric[1] + electric[2] * electric[2]
            )
            electric = displace / (perm_local + chi_local * energy)[None]
    first = reach + ADVANCE
    final = reach + planes_dev + ADVANCE
    row_lo = STEPS
    row_hi = STEPS + rows_dev
    d_out = displace[:, first:final, row_lo:row_hi]
    e_out = electric[:, first:final, row_lo:row_hi]
    h_out = magnetic[:, first:final, row_lo:row_hi]
    eps_keep = padded[9, first : final - ADVANCE, row_lo:row_hi]
    chi_keep = padded[10, first : final - ADVANCE, row_lo:row_hi]
    eps_tail = padded[9, final - ADVANCE : final, row_lo:row_hi]
    chi_tail = padded[10, final - ADVANCE : final, row_lo:row_hi]
    eps_tail = jnp.where(is_last, lookup(classes, eps_table), eps_tail)
    chi_tail = jnp.where(is_last, lookup(classes, chi_table), chi_tail)
    eps_out = jnp.concatenate([eps_keep, eps_tail], axis=0)
    chi_out = jnp.concatenate([chi_keep, chi_tail], axis=0)
    return (d_out, e_out, h_out, eps_out, chi_out)


def solution(mesh):
    placed = (
        P(None, "gz", "gx", None),
        P(None, "gz", "gx", None),
        P(None, "gz", "gx", None),
        P("gz", "gx", None),
        P("gz", "gx", None),
        P(None, "gx", None),
        P(),
        P(),
    )
    return jax.shard_map(
        on_device,
        mesh=mesh,
        in_specs=placed,
        out_specs=(
            P(None, "gz", "gx", None),
            P(None, "gz", "gx", None),
            P(None, "gz", "gx", None),
            P("gz", "gx", None),
            P("gz", "gx", None),
        ),
        check_vma=False,
    )
```

profile of v0, /device:TPU:9, one launch (start us, length us, event | category | flops | bytes accessed | tf_op | source)
XLA Modules:
  0.0 88.0 jit_solution(7506662286053926142)
XLA Ops:
  0.7 1.1 %constant_dynamic-update-slice_fusion.4 = f32[11,8,32,128]{3,2,1,0:T(8,128)S(1)} fusion(f32[3,8,32,128]{3,2,1,0:T(8,128)} %param.8), kind=kLoop, calls=%fused_computation.189 | loop fusion | bytes 786432
  1.7 1.0 %constant_dynamic-update-slice_fusion.3 = f32[11,8,32,128]{3,2,1,0:T(8,128)S(1)} fusion(f32[11,8,32,128]{3,2,1,0:T(8,128)S(1)} %constant_dynamic-update-slice_fusion.4, f32[3,8,32,128]{3,2,1,0:T(8,128)} %param.9), kind=kLoop, calls=%fused_computation.188 | loop fusion | bytes 786432
  2.9 1.7 %fusion.61 = (f32[11,6,32,128]{3,2,1,0:T(8,128)}, f32[11,6,32,128]{3,2,1,0:T(8,128)}) fusion(f32[11,8,32,128]{3,2,1,0:T(8,128)S(1)} %constant_dynamic-update-slice_fusion), kind=kLoop, calls=%fused_computation.194 | loop fusion | bytes 4325376 | tf_op jit(solution)/shard_map/slice | solution.py:19
  4.5 3.1 %collective-permute-start = (f32[11,6,32,128]{3,2,1,0:T(8,128)}, f32[11,6,32,128]{3,2,1,0:T(8,128)}, u32[]{:S(2)}, u32[]{:S(2)}) collective-permute-start(f32[11,6,32,128]{3,2,1,0:T(8,128)} %get-tuple-element.27), channel_id=1, source_target_pairs={{0,4},{4,8},{8,12},{12,16},{16,20},{20,24},{24,28},{1,5},{5,9},{9,... | collective-permute-start | bytes 3244040 | tf_op jit(solution)/shard_map/ppermute | solution.py:22
  7.7 3.1 %collective-permute-start.1 = (f32[11,6,32,128]{3,2,1,0:T(8,128)}, f32[11,6,32,128]{3,2,1,0:T(8,128)S(1)}, u32[]{:S(2)}, u32[]{:S(2)}) collective-permute-start(f32[11,6,32,128]{3,2,1,0:T(8,128)} %get-tuple-element.28), channel_id=1, source_target_pairs={{4,0},{8,4},{12,8},{16,12},{20,16},{24,20},{28,24},{5,1},{9,5},{13... | collective-permute-start | bytes 3244040 | tf_op jit(solution)/shard_map/ppermute | solution.py:24
  10.9 42.8 %collective-permute-done = f32[11,6,32,128]{3,2,1,0:T(8,128)} collective-permute-done((f32[11,6,32,128]{3,2,1,0:T(8,128)}, f32[11,6,32,128]{3,2,1,0:T(8,128)}, u32[]{:S(2)}, u32[]{:S(2)}) %collective-permute-start) | collective-permute-done | bytes 1081376 | tf_op jit(solution)/shard_map/ppermute | solution.py:22
  53.7 2.8 %collective-permute-done.1 = f32[11,6,32,128]{3,2,1,0:T(8,128)S(1)} collective-permute-done((f32[11,6,32,128]{3,2,1,0:T(8,128)}, f32[11,6,32,128]{3,2,1,0:T(8,128)S(1)}, u32[]{:S(2)}, u32[]{:S(2)}) %collective-permute-start.1) | collective-permute-done | bytes 1081376 | tf_op jit(solution)/shard_map/ppermute | solution.py:24
  56.5 1.2 %pad_maximum_fusion.3 = (f32[11,20,4,128]{3,2,1,0:T(4,128)S(1)}, f32[11,20,4,128]{3,2,1,0:T(4,128)S(1)}) fusion(f32[11,6,32,128]{3,2,1,0:T(8,128)S(1)} %collective-permute-done.1, f32[11,8,32,128]{3,2,1,0:T(8,128)S(1)} %constant_dynamic-update-slice_fusion, f32[11,6,32,128]{3,2,1,0:T(8,128)} %collective-permute-done), kind=kLoop, calls=%fused_computation.38 | loop fusion | flops 450560 | bytes 4505600 | tf_op jit(solution)/shard_map/slice | solution.py:19
  57.7 3.5 %collective-permute-start.2 = (f32[11,20,4,128]{3,2,1,0:T(4,128)S(1)}, f32[11,20,4,128]{3,2,1,0:T(4,128)S(1)}, u32[]{:S(2)}, u32[]{:S(2)}) collective-permute-start(f32[11,20,4,128]{3,2,1,0:T(4,128)S(1)} %get-tuple-element.25), channel_id=1, source_target_pairs={{0,1},{1,2},{2,3},{4,5},{5,6},{6,7},{8,9},{9,10},{10,11},{12,13},{... | collective-permute-start | bytes 1351688 | tf_op jit(solution)/shard_map/ppermute | solution.py:22
  61.2 1.9 %collective-permute-start.3 = (f32[11,20,4,128]{3,2,1,0:T(4,128)S(1)}, f32[11,20,4,128]{3,2,1,0:T(4,128)S(1)}, u32[]{:S(2)}, u32[]{:S(2)}) collective-permute-start(f32[11,20,4,128]{3,2,1,0:T(4,128)S(1)} %get-tuple-element.26), channel_id=1, source_target_pairs={{1,0},{2,1},{3,2},{5,4},{6,5},{7,6},{9,8},{10,9},{11,10},{13,12},{... | collective-permute-start | bytes 1351688 | tf_op jit(solution)/shard_map/ppermute | solution.py:24
  63.3 0.7 pad_maximum_fusion.7
  64.0 2.5 %collective-permute-done.2 = f32[11,20,4,128]{3,2,1,0:T(4,128)S(1)} collective-permute-done((f32[11,20,4,128]{3,2,1,0:T(4,128)S(1)}, f32[11,20,4,128]{3,2,1,0:T(4,128)S(1)}, u32[]{:S(2)}, u32[]{:S(2)}) %collective-permute-start.2) | collective-permute-done | bytes 450592 | tf_op jit(solution)/shard_map/ppermute | solution.py:22
  66.5 4.4 %collective-permute-done.3 = f32[11,20,4,128]{3,2,1,0:T(4,128)S(1)} collective-permute-done((f32[11,20,4,128]{3,2,1,0:T(4,128)S(1)}, f32[11,20,4,128]{3,2,1,0:T(4,128)S(1)}, u32[]{:S(2)}, u32[]{:S(2)}) %collective-permute-start.3) | collective-permute-done | bytes 450592 | tf_op jit(solution)/shard_map/ppermute | solution.py:24
  70.9 1.5 %add_bitcast_fusion.3 = (f32[20,40,128]{2,1,0:T(8,128)S(1)}, f32[1,20,40,128]{3,2,1,0:T(8,128)S(1)}, f32[1,20,40,128]{3,2,1,0:T(8,128)S(1)}, f32[1,20,40,128]{3,...) fusion(f32[20,40]{1,0:T(8,128)S(1)} %get-tuple-element.94, ...), kind=kLoop, calls=%fused_computation.141 | loop fusion | flops 2969600 | bytes 6967200 | tf_op jit(solution)/shard_map/div | solution.py:93
  72.5 0.2 slice.652
  72.6 0.2 slice.655
  72.8 1.0 %maximum_bitcast_fusion.1 = (f32[19,40,128]{2,1,0:T(8,128)S(1)}, f32[19,40,128]{2,1,0:T(8,128)S(1)}) fusion(f32[11,20,4,128]{3,2,1,0:T(4,128)S(1)} %collective-permute-done.3, f32[11,20,4,128]{3,2,1,0:T(4,128)S(1)} %collective-permute-done.2, f32[11,6,32,128]{3,2,1,0:T(8,128)S(1)} %collective-permute-done.1, ...), kind=kLoop, calls=%fused_computation.163 | loop fusion | flops 778240 | bytes 5283840 | tf_op jit(solution)/shard_map/slice | solution.py:33
  73.9 0.2 subtract_bitcast_fusion.23
  74.1 1.9 %pad_maximum_fusion = f32[11,20,40,128]{3,2,1,0:T(8,128)S(1)} fusion(f32[11,20,4,128]{3,2,1,0:T(4,128)S(1)} %collective-permute-done.3, f32[11,6,32,128]{3,2,1,0:T(8,128)S(1)} %collective-permute-done.1, f32[11,8,32,128]{3,2,1,0:T(8,128)S(1)} %constant_dynamic-update-slice_fusion, f32[11,6,32,128]{3,2,1,0:T(8,128)} %collective-permute-done, ...), kind=kLoop, calls=%fused_computation | loop fusion | flops 4505600 | bytes 9011200 | tf_op jit(solution)/shard_map/concatenate | solution.py:20
  76.0 0.2 fusion
  76.4 0.5 subtract_bitcast_fusion.20
  76.9 0.3 broadcast_divide_fusion.10
  77.7 0.2 slice_bitcast_fusion.34
  78.0 0.2 slice.672
  78.1 0.2 slice.679
  78.3 0.2 subtract_bitcast_fusion.17
  78.5 0.3 fusion.3
  79.0 0.5 subtract_bitcast_fusion.14
  79.5 0.3 broadcast_divide_fusion.7
  79.8 0.2 fusion.42
  80.0 0.2 fusion.37
  80.4 0.2 slice_bitcast_fusion.31
  80.6 0.2 slice.696
  80.8 0.2 slice.703
  81.0 0.2 subtract_bitcast_fusion.11
  81.2 0.5 fusion.7
  81.8 0.5 subtract_bitcast_fusion.8
  82.3 0.3 broadcast_divide_fusion.4
  82.6 0.2 fusion.32
  83.2 0.2 slice_bitcast_fusion.28
  83.4 0.2 slice.720
  83.6 0.2 slice.727
  83.8 0.2 subtract_bitcast_fusion.5
  84.1 0.8 fusion.11
  84.9 0.8 slice.746
  85.8 0.4 subtract_bitcast_fusion.2
  86.3 0.3 broadcast_divide_fusion.1
  87.0 1.0 %broadcast_divide_fusion.11 = (f32[3,8,32,128]{3,2,1,0:T(8,128)}, f32[3,8,32,128]{3,2,1,0:T(8,128)}) fusion(f32[8,32,128]{2,1,0:T(8,128)S(1)} %slice.745, f32[3,20,40,128]{3,2,1,0:T(8,128)S(1)} %get-tuple-element.10), kind=kLoop, calls=%fused_computation.176 | loop fusion | flops 98304 | bytes 1310720 | tf_op jit(solution)/shard_map/div | solution.py:93
  (54 shorter events, 2.8 us)
Async XLA Ops:
  0.6 2.1 %copy-start.2 = (f32[3,8,32,128]{3,2,1,0:T(8,128)S(1)}, f32[3,8,32,128]{3,2,1,0:T(8,128)}, u32[]{:S(2)}) copy-start(f32[3,8,32,128]{3,2,1,0:T(8,128)} %param.10) | copy-start | bytes 1179652
  0.6 2.2 %copy-start.1 = (f32[8,32,128]{2,1,0:T(8,128)S(1)}, f32[8,32,128]{2,1,0:T(8,128)}, u32[]{:S(2)}) copy-start(f32[8,32,128]{2,1,0:T(8,128)} %param.11) | copy-start | bytes 393220
  0.7 2.2 %copy-start = (f32[8,32,128]{2,1,0:T(8,128)S(1)}, f32[8,32,128]{2,1,0:T(8,128)}, u32[]{:S(2)}) copy-start(f32[8,32,128]{2,1,0:T(8,128)} %param.12) | copy-start | bytes 393220
  4.5 49.1 %collective-permute-start = (f32[11,6,32,128]{3,2,1,0:T(8,128)}, f32[11,6,32,128]{3,2,1,0:T(8,128)}, u32[]{:S(2)}, u32[]{:S(2)}) collective-permute-start(f32[11,6,32,128]{3,2,1,0:T(8,128)} %get-tuple-element.27), channel_id=1, source_target_pairs={{0,4},{4,8},{8,12},{12,16},{16,20},{20,24},{24,28},{1,5},{5,9},{9,... | collective-permute-start | bytes 3244040 | tf_op jit(solution)/shard_map/ppermute | solution.py:22
  7.7 48.8 %collective-permute-start.1 = (f32[11,6,32,128]{3,2,1,0:T(8,128)}, f32[11,6,32,128]{3,2,1,0:T(8,128)S(1)}, u32[]{:S(2)}, u32[]{:S(2)}) collective-permute-start(f32[11,6,32,128]{3,2,1,0:T(8,128)} %get-tuple-element.28), channel_id=1, source_target_pairs={{4,0},{8,4},{12,8},{16,12},{20,16},{24,20},{28,24},{5,1},{9,5},{13... | collective-permute-start | bytes 3244040 | tf_op jit(solution)/shard_map/ppermute | solution.py:24
  10.9 52.3 %copy-start.3 = (s32[2,32,128]{2,1,0:T(8,128)S(1)}, s32[2,32,128]{2,1,0:T(8,128)}, u32[]{:S(2)}) copy-start(s32[2,32,128]{2,1,0:T(8,128)} %param.13) | copy-start | bytes 98308
  10.9 52.3 %copy-start.4 = (f32[8]{0:T(128)S(1)}, f32[8]{0:T(128)}, u32[]{:S(2)}) copy-start(f32[8]{0:T(128)} %param.15) | copy-start | bytes 100
  10.9 52.3 %copy-start.5 = (f32[8]{0:T(128)S(1)}, f32[8]{0:T(128)}, u32[]{:S(2)}) copy-start(f32[8]{0:T(128)} %param.14) | copy-start | bytes 100
  57.7 8.8 %collective-permute-start.2 = (f32[11,20,4,128]{3,2,1,0:T(4,128)S(1)}, f32[11,20,4,128]{3,2,1,0:T(4,128)S(1)}, u32[]{:S(2)}, u32[]{:S(2)}) collective-permute-start(f32[11,20,4,128]{3,2,1,0:T(4,128)S(1)} %get-tuple-element.25), channel_id=1, source_target_pairs={{0,1},{1,2},{2,3},{4,5},{5,6},{6,7},{8,9},{9,10},{10,11},{12,13},{... | collective-permute-start | bytes 1351688 | tf_op jit(solution)/shard_map/ppermute | solution.py:22
  61.2 9.7 %collective-permute-start.3 = (f32[11,20,4,128]{3,2,1,0:T(4,128)S(1)}, f32[11,20,4,128]{3,2,1,0:T(4,128)S(1)}, u32[]{:S(2)}, u32[]{:S(2)}) collective-permute-start(f32[11,20,4,128]{3,2,1,0:T(4,128)S(1)} %get-tuple-element.26), channel_id=1, source_target_pairs={{1,0},{2,1},{3,2},{5,4},{6,5},{7,6},{9,8},{10,9},{11,10},{13,12},{... | collective-permute-start | bytes 1351688 | tf_op jit(solution)/shard_map/ppermute | solution.py:24
where the time goes:
time: 88.3 us; the launch traced here: 88 us
  waiting for transfers between devices  52.5 us (59%)
  other arithmetic  15.7 us (18%)
  starting transfers between devices  11.6 us (13%)
  local copies, waits for them, and re-layouts  7.01 us (8%)
  between operations  1.16 us (1%)
    ppermute x2, waiting for transfers between devices, with_halo(): lax.ppermute(tail, axis, [(i, (i + 1) % count) for i in range(ends)])  45.2 us
    ppermute x2, waiting for transfers between devices, with_halo(): lax.ppermute(head, axis, [((i + 1) % count, i) for i in range(ends)])  7.23 us
    ppermute x2, starting transfers between devices, with_halo(): lax.ppermute(tail, axis, [(i, (i + 1) % count) for i in range(ends)])  6.64 us
    div x21, other arithmetic, on_device(): electric = displace / (perm_local + chi_local * energy)[None]  5.52 us
    ppermute x2, starting transfers between devices, with_halo(): lax.ppermute(head, axis, [((i + 1) % count, i) for i in range(ends)])  4.98 us
    unnamed x16, local copies, waits for them, and re-layouts  2.18 us
    concatenate x1, other arithmetic, with_halo(): jnp.concatenate([lax.ppermute(tail, axis, [(i, (i + 1) % count) for i in...  1.93 us
    another operation x4, other arithmetic, local_curl_behind(): return jnp.stack([curl_x, curl_y, curl_z])  1.88 us
  transfers between devices with their start and end apart: 4, of which 4 were waited for; matrix products, arithmetic and copies ran while one was open for 1% of the time, Pallas kernels for 0%

commit v1 on v0

v1 whole, which is shorter than its diff:
```python
import functools

import jax
import jax.numpy as jnp
from jax import lax
from jax.experimental import pallas as pl
from jax.experimental.pallas import tpu as pltpu
from jax.sharding import PartitionSpec as P

STEPS = 4
KERR = 3
ADVANCE = 2
COURANT = 0.5
LOW = STEPS - ADVANCE
HALO = STEPS
MESH = pl.DeviceIdType.MESH


def kernel(
    gz_name, gx_name, gz_count, gx_count,
    d_in, e_in, h_in, eps_in, chi_in, cls_ref, eps_tab, chi_tab,
    d_out, e_out, h_out, eps_out, chi_out,
    F, EX, SE, SU, SL, RU, RL, load_sem, send_sem, recv_sem,
):
    planes, rows, lanes = d_in.shape[1], d_in.shape[2], d_in.shape[3]
    wide = rows + 2 * HALO
    gz = lax.axis_index(gz_name)
    gx = lax.axis_index(gx_name)
    has_dn, has_up = gz > 0, gz < gz_count - 1
    has_lf, has_rt = gx > 0, gx < gx_count - 1
    own = pl.ds(0, rows)
    every = pl.ds(LOW, planes)

    loads = [
        pltpu.make_async_copy(src, F.at[at, every, own], load_sem.at[i])
        for i, (src, at) in enumerate(
            [
                (e_in, pl.ds(0, 3)),
                (h_in, pl.ds(3, 3)),
                (d_in, pl.ds(6, 3)),
                (eps_in, 9),
                (chi_in, 10),
            ]
        )
    ]
    for c in loads:
        c.start()

    barrier = pltpu.get_barrier_semaphore()
    around = []
    for dz in (-1, 0, 1):
        for dx in (-1, 0, 1):
            if dz == 0 and dx == 0:
                continue
            cond = None
            for d, lo, hi in ((dz, has_dn, has_up), (dx, has_lf, has_rt)):
                if d:
                    c = lo if d < 0 else hi
                    cond = c if cond is None else jnp.logical_and(cond, c)
            around.append(((dz, dx), cond))
    conds = dict(around)
    total = jnp.int32(0)
    for (dz, dx), cond in around:
        @pl.when(cond)
        def _(dz=dz, dx=dx):
            pl.semaphore_signal(barrier, inc=1, device_id=(gz + dz, gx + dx), device_id_type=MESH)
        total = total + jnp.where(cond, 1, 0).astype(jnp.int32)
    pl.semaphore_wait(barrier, total)

    n_copy = [0]

    def remote(src, dst, dz, dx):
        i = n_copy[0]
        n_copy[0] += 1
        copy = pltpu.make_async_remote_copy(
            src_ref=src, dst_ref=dst, send_sem=send_sem.at[i], recv_sem=recv_sem.at[i],
            device_id=(gz + dz, gx + dx), device_id_type=MESH,
        )
        return copy, conds[(dz, dx)], conds[(-dz, -dx)]

    def start(group):
        for copy, to, _ in group:
            pl.when(to)(copy.start)

    def arrive(group):
        for copy, _, frm in group:
            pl.when(frm)(copy.wait_recv)

    def sent(group):
        for copy, to, _ in group:
            pl.when(to)(copy.wait_send)

    top = LOW + planes
    last = pl.ds(planes - LOW, LOW)
    up_main = [
        remote(e_in.at[:, last], F.at[pl.ds(0, 3), pl.ds(0, LOW), own], 1, 0),
        remote(h_in.at[:, last], F.at[pl.ds(3, 3), pl.ds(0, LOW), own], 1, 0),
        remote(d_in.at[:, planes - 1], F.at[pl.ds(6, 3), LOW - 1, own], 1, 0),
        remote(eps_in.at[planes - 1], F.at[9, LOW - 1, own], 1, 0),
        remote(chi_in.at[planes - 1], F.at[10, LOW - 1, own], 1, 0),
    ]
    first = pl.ds(0, ADVANCE)
    above = pl.ds(top, ADVANCE)
    dn_main = [
        remote(e_in.at[:, first], F.at[pl.ds(0, 3), above, own], -1, 0),
        remote(h_in.at[:, first], F.at[pl.ds(3, 3), above, own], -1, 0),
        remote(d_in.at[:, first], F.at[pl.ds(6, 3), above, own], -1, 0),
        remote(eps_in.at[first], F.at[9, above, own], -1, 0),
        remote(chi_in.at[first], F.at[10, above, own], -1, 0),
        remote(e_in.at[pl.ds(0, 2), ADVANCE], EX.at[0, :, own], -1, 0),
    ]
    side, up_diag, dn_diag = [], [], []
    for S, R, dx in ((SU, RU, -1), (SL, RL, 1)):
        side.append(remote(S, R.at[:, every], 0, dx))
        up_diag.append(remote(S.at[:, planes - 1], R.at[:, LOW - 1], 1, dx))
        up_diag.append(
            remote(S.at[pl.ds(0, 5), pl.ds(planes - LOW, LOW - 1)], R.at[pl.ds(0, 5), pl.ds(0, LOW - 1)], 1, dx)
        )
        dn_diag.append(remote(S.at[:, first], R.at[:, above], -1, dx))
        dn_diag.append(remote(S.at[pl.ds(0, 2), ADVANCE], R.at[pl.ds(0, 2), top + ADVANCE], -1, dx))
    e_down = [remote(SE.at[s], EX.at[s + 1], -1, 0) for s in range(STEPS - 1)]

    start(up_main)
    for c in loads:
        c.wait()

    def stage(p, carry):
        SU[:, p] = F[:, p + LOW, 0:HALO, :]
        SL[:, p] = F[:, p + LOW, rows - HALO : rows, :]
        return carry

    lax.fori_loop(0, planes, stage, 0)
    start(side)
    start(up_diag)
    start(dn_main)
    start(dn_diag)

    is_top = jnp.logical_not(has_up)

    @pl.when(is_top)
    def _():
        zero = jnp.zeros((wide, lanes), jnp.float32)
        for c in range(2):
            for s in range(STEPS):
                EX[s, c] = zero
        for q in range(ADVANCE):
            cls = cls_ref[q]
            for at, tab in ((9, eps_tab), (10, chi_tab)):
                val = jnp.zeros(cls.shape, jnp.float32)
                for k in range(tab.shape[0]):
                    val = jnp.where(cls == k, tab[k], val)
                F[at, top + q, 0:rows, :] = val
            for c in range(9):
                F[c, top + q, 0:rows, :] = jnp.zeros((rows, lanes), jnp.float32)

    def join(q, count):
        F[0:count, q, rows : rows + HALO, :] = jnp.where(has_rt, RU[0:count, q], 0.0)
        F[0:count, q, rows + HALO : wide, :] = jnp.where(has_lf, RL[0:count, q], 0.0)

    row = lax.broadcasted_iota(jnp.int32, (wide, lanes), 0)
    lane = lax.broadcasted_iota(jnp.int32, (wide, lanes), 1)
    h_off = jnp.logical_and(row >= rows + HALO, jnp.logical_not(has_lf))
    e_off = jnp.logical_and(jnp.logical_and(row >= rows, row < rows + HALO), jnp.logical_not(has_rt))
    lane_end = lane == lanes - 1
    lane_start = lane == 0

    def y_next(v):
        return jnp.where(lane_end, 0.0, pltpu.roll(v, lanes - 1, 1))

    def y_prev(v):
        return jnp.where(lane_start, 0.0, pltpu.roll(v, 1, 1))

    def x_next(v):
        return pltpu.roll(v, wide - 1, 0)

    def x_prev(v):
        return pltpu.roll(v, 1, 0)

    def h_update(q, e_above):
        ex, ey, ez = F[0, q], F[1, q], F[2, q]
        ax, ay = e_above
        off = h_off
        below = jnp.logical_and(q < LOW, jnp.logical_not(has_dn))
        off = jnp.logical_or(off, below)
        hx = F[3, q] - COURANT * ((y_next(ez) - ez) - (ay - ey))
        hy = F[4, q] - COURANT * ((ax - ex) - (x_next(ez) - ez))
        hz = F[5, q] - COURANT * ((x_next(ey) - ey) - (y_next(ex) - ex))
        hx = jnp.where(off, 0.0, hx)
        hy = jnp.where(off, 0.0, hy)
        hz = jnp.where(off, 0.0, hz)
        F[3, q] = hx
        F[4, q] = hy
        F[5, q] = hz
        return (ex, ey, ez), (hx, hy, hz)

    def plane_update(q, e_above, outside):
        (ex, ey, ez), (hx, hy, hz) = h_update(q, e_above)
        bx, by = F[3, q - 1], F[4, q - 1]
        dx = F[6, q] + COURANT * ((hz - y_prev(hz)) - (hy - by))
        dy = F[7, q] + COURANT * ((hx - bx) - (hz - x_prev(hz)))
        dz = F[8, q] + COURANT * ((hy - x_prev(hy)) - (hx - y_prev(hx)))
        F[6, q] = dx
        F[7, q] = dy
        F[8, q] = dz
        eps, chi = F[9, q], F[10, q]
        for _ in range(KERR):
            inv = 1.0 / (eps + chi * (ex * ex + ey * ey + ez * ez))
            ex, ey, ez = dx * inv, dy * inv, dz * inv
        off = jnp.logical_or(e_off, outside)
        F[0, q] = jnp.where(off, 0.0, ex)
        F[1, q] = jnp.where(off, 0.0, ey)
        F[2, q] = jnp.where(off, 0.0, ez)

    def from_above(q):
        return F[0, q + 1], F[1, q + 1]

    def sweep(q, carry):
        plane_update(q, from_above(q), jnp.logical_and(q >= top, is_top))
        return carry

    arrive(side)

    def join_own(q, carry):
        join(q, 11)
        return carry

    lax.fori_loop(LOW, top, join_own, 0)
    arrive(up_main)
    arrive(up_diag)
    for q in range(LOW - 1):
        join(q, 5)
    join(LOW - 1, 11)

    for s in range(1, STEPS + 1):
        h_update(s - 1, from_above(s - 1))
        lax.fori_loop(s, top - s, sweep, 0)
        if s < STEPS:
            SE[s - 1] = F[0:2, LOW + ADVANCE]
            start(e_down[s - 1 : s])

    arrive(dn_main)
    arrive(dn_diag)
    for q in range(ADVANCE):
        join(top + q, 11)
    EX[0, :, rows : rows + HALO, :] = jnp.where(has_rt, RU[0:2, top + ADVANCE], 0.0)
    EX[0, :, rows + HALO : wide, :] = jnp.where(has_lf, RL[0:2, top + ADVANCE], 0.0)

    @pl.when(is_top)
    def _():
        for c in range(9):
            for q in range(ADVANCE):
                F[c, top + q] = jnp.zeros((wide, lanes), jnp.float32)
        EX[0] = jnp.zeros((2, wide, lanes), jnp.float32)

    for s in range(1, STEPS + 1):
        lax.fori_loop(top - s, top + ADVANCE - 1, sweep, 0)
        if s > 1:
            arrive(e_down[s - 2 : s - 1])
        q = top + ADVANCE - 1
        plane_update(q, (EX[s - 1, 0], EX[s - 1, 1]), is_top)

    @pl.when(is_top)
    def _():
        for c in range(3, 9):
            for q in range(ADVANCE):
                F[c, top + q] = jnp.zeros((wide, lanes), jnp.float32)

    moved = pl.ds(LOW + ADVANCE, planes)
    stores = [
        pltpu.make_async_copy(F.at[at, moved, own], dst, load_sem.at[i])
        for i, (dst, at) in enumerate(
            [
                (e_out, pl.ds(0, 3)),
                (h_out, pl.ds(3, 3)),
                (d_out, pl.ds(6, 3)),
                (eps_out, 9),
                (chi_out, 10),
            ]
        )
    ]
    for c in stores:
        c.start()
    for group in (up_main, side, up_diag, dn_main, dn_diag, e_down):
        sent(group)
    for c in stores:
        c.wait()


N_COPIES = 5 + 6 + 10 + STEPS - 1


def on_device(mesh, d_field, e_field, h_field, permittivity, kerr_coeff, classes, eps_table, chi_table):
    gz_name, gx_name = mesh.axis_names
    _, planes, rows, lanes = d_field.shape
    wide = rows + 2 * HALO
    depth = LOW + planes + ADVANCE
    f32 = jnp.float32
    hbm = pl.BlockSpec(memory_space=pl.ANY)
    smem = pl.BlockSpec(memory_space=pltpu.SMEM)
    vmem = pl.BlockSpec(memory_space=pltpu.VMEM)
    return pl.pallas_call(
        functools.partial(kernel, gz_name, gx_name, mesh.shape[gz_name], mesh.shape[gx_name]),
        out_shape=[jax.ShapeDtypeStruct(a.shape, f32) for a in (d_field, e_field, h_field, permittivity, kerr_coeff)],
        in_specs=[hbm] * 5 + [vmem, smem, smem],
        out_specs=[hbm] * 5,
        scratch_shapes=[
            pltpu.VMEM((11, depth, wide, lanes), f32),
            pltpu.VMEM((STEPS, 2, wide, lanes), f32),
            pltpu.VMEM((STEPS - 1, 2, wide, lanes), f32),
            pltpu.VMEM((11, planes, HALO, lanes), f32),
            pltpu.VMEM((11, planes, HALO, lanes), f32),
            pltpu.VMEM((11, depth + 1, HALO, lanes), f32),
            pltpu.VMEM((11, depth + 1, HALO, lanes), f32),
            pltpu.SemaphoreType.DMA((5,)),
            pltpu.SemaphoreType.DMA((N_COPIES,)),
            pltpu.SemaphoreType.DMA((N_COPIES,)),
        ],
        compiler_params=pltpu.CompilerParams(
            collective_id=0, has_side_effects=True, vmem_limit_bytes=32 * 1024 * 1024
        ),
        name="window",
    )(d_field, e_field, h_field, permittivity, kerr_coeff, classes, eps_table, chi_table)


def solution(mesh):
    field = P(None, "gz", "gx", None)
    cell = P("gz", "gx", None)
    return jax.shard_map(
        functools.partial(on_device, mesh),
        mesh=mesh,
        in_specs=(field, field, field, cell, cell, P(None, "gx", None), P(), P()),
        out_specs=(field, field, field, cell, cell),
        check_vma=False,
    )
```

time: 88.3 us -> 44.7 us (0.51)
  the two profiles are of different devices: /device:TPU:9 before, /device:TPU:0 now
where the time goes in v1:
time: 44.7 us; the launch traced here: 44.4 us
  Pallas kernels  33.3 us (74%)
  local copies, waits for them, and re-layouts  10.4 us (23%)
  between operations  0.66 us (1%)
    pallas_call x1, Pallas kernels, on_device(): pl.pallas_call(functools.partial(kernel, gz_name, gx_name, mesh.shape[gz_...  33.3 us
    unnamed x21, local copies, waits for them, and re-layouts  10.4 us

profile of v1, /device:TPU:0, one launch (start us, length us, event | category | flops | bytes accessed | tf_op | source)
XLA Modules:
  0.0 44.4 jit_solution(13745687551999645943)
XLA Ops:
  0.6 0.0 copy-start
  0.6 1.0 %copy-done = f32[3,8,32,128]{3,2,1,0:T(8,128)S(1)} copy-done((f32[3,8,32,128]{3,2,1,0:T(8,128)S(1)}, f32[3,8,32,128]{3,2,1,0:T(8,128)}, u32[]{:S(2)}) %copy-start) | copy-done | bytes 393240
  1.6 0.0 copy-start.1
  1.6 1.0 %copy-done.1 = f32[3,8,32,128]{3,2,1,0:T(8,128)S(1)} copy-done((f32[3,8,32,128]{3,2,1,0:T(8,128)S(1)}, f32[3,8,32,128]{3,2,1,0:T(8,128)}, u32[]{:S(2)}) %copy-start.1) | copy-done | bytes 393240
  2.6 0.0 copy-start.2
  2.6 1.0 %copy-done.2 = f32[3,8,32,128]{3,2,1,0:T(8,128)S(1)} copy-done((f32[3,8,32,128]{3,2,1,0:T(8,128)S(1)}, f32[3,8,32,128]{3,2,1,0:T(8,128)}, u32[]{:S(2)}) %copy-start.2) | copy-done | bytes 393240
  3.6 0.0 copy-start.3
  3.6 0.9 %copy-done.3 = f32[8,32,128]{2,1,0:T(8,128)S(1)} copy-done((f32[8,32,128]{2,1,0:T(8,128)S(1)}, f32[8,32,128]{2,1,0:T(8,128)}, u32[]{:S(2)}) %copy-start.3) | copy-done | bytes 131096
  4.5 0.0 copy-start.4
  4.5 0.9 %copy-done.4 = f32[8,32,128]{2,1,0:T(8,128)S(1)} copy-done((f32[8,32,128]{2,1,0:T(8,128)S(1)}, f32[8,32,128]{2,1,0:T(8,128)}, u32[]{:S(2)}) %copy-start.4) | copy-done | bytes 131096
  5.4 0.0 copy-start.5
  5.4 0.8 %copy-done.5 = s32[2,32,128]{2,1,0:T(8,128)S(1)} copy-done((s32[2,32,128]{2,1,0:T(8,128)S(1)}, s32[2,32,128]{2,1,0:T(8,128)}, u32[]{:S(2)}) %copy-start.5) | copy-done | bytes 32792
  6.2 0.0 copy-start.6
  6.2 0.7 %copy-done.6 = f32[8]{0:T(128)S(1)} copy-done((f32[8]{0:T(128)S(1)}, f32[8]{0:T(128)}, u32[]{:S(2)}) %copy-start.6) | copy-done | bytes 56
  6.8 0.0 copy-start.7
  6.8 0.7 %copy-done.7 = f32[8]{0:T(128)S(1)} copy-done((f32[8]{0:T(128)S(1)}, f32[8]{0:T(128)}, u32[]{:S(2)}) %copy-start.7) | copy-done | bytes 56
  7.5 33.3 %window.1 = (f32[3,8,32,128]{3,2,1,0:T(8,128)S(1)}, f32[3,8,32,128]{3,2,1,0:T(8,128)S(1)}, f32[3,8,32,128]{3,2,1,0:T(8,128)S(1)}, f32[8,32,128]{2,1,0:T(8,128)S(1)}, f32[8,32,128]{2,1,0:T(8,128)S(1)}) custom-call(f32[3,8,32,128]{3,2,1,0:T(8,128)S(1)} %copy-done, f32[3,8,32,128]{3,2,1,0:T(8,128)S(1)} %copy-done.1, f32[3,8,32,128]{3,2,1,0:T(8,128)S(1)} %copy-done.2, ...), custom_call_target="tpu_custom_call" | custom-call | tf_op jit(solution)/shard_map/window/pallas_call | solution.py:301
  40.8 0.7 %copy.18 = f32[3,8,32,128]{3,2,1,0:T(8,128)} copy(f32[3,8,32,128]{3,2,1,0:T(8,128)S(1)} %get-tuple-element.10) | data formatting | bytes 786432
  41.6 0.7 %copy.19 = f32[3,8,32,128]{3,2,1,0:T(8,128)} copy(f32[3,8,32,128]{3,2,1,0:T(8,128)S(1)} %get-tuple-element.11) | data formatting | bytes 786432
  42.3 0.7 %copy.20 = f32[3,8,32,128]{3,2,1,0:T(8,128)} copy(f32[3,8,32,128]{3,2,1,0:T(8,128)S(1)} %get-tuple-element.12) | data formatting | bytes 786432
  43.1 0.7 %copy.21 = f32[8,32,128]{2,1,0:T(8,128)} copy(f32[8,32,128]{2,1,0:T(8,128)S(1)} %get-tuple-element.13) | data formatting | bytes 262144
  43.7 0.7 %copy.22 = f32[8,32,128]{2,1,0:T(8,128)} copy(f32[8,32,128]{2,1,0:T(8,128)S(1)} %get-tuple-element.14) | data formatting | bytes 262144
Async XLA Ops:
  0.6 1.0 %copy-start = (f32[3,8,32,128]{3,2,1,0:T(8,128)S(1)}, f32[3,8,32,128]{3,2,1,0:T(8,128)}, u32[]{:S(2)}) copy-start(f32[3,8,32,128]{3,2,1,0:T(8,128)} %d_in.1) | copy-start | bytes 1179652
  1.6 1.0 %copy-start.1 = (f32[3,8,32,128]{3,2,1,0:T(8,128)S(1)}, f32[3,8,32,128]{3,2,1,0:T(8,128)}, u32[]{:S(2)}) copy-start(f32[3,8,32,128]{3,2,1,0:T(8,128)} %e_in.1) | copy-start | bytes 1179652
  2.6 1.0 %copy-start.2 = (f32[3,8,32,128]{3,2,1,0:T(8,128)S(1)}, f32[3,8,32,128]{3,2,1,0:T(8,128)}, u32[]{:S(2)}) copy-start(f32[3,8,32,128]{3,2,1,0:T(8,128)} %h_in.1) | copy-start | bytes 1179652
  3.6 0.9 %copy-start.3 = (f32[8,32,128]{2,1,0:T(8,128)S(1)}, f32[8,32,128]{2,1,0:T(8,128)}, u32[]{:S(2)}) copy-start(f32[8,32,128]{2,1,0:T(8,128)} %eps_in.1) | copy-start | bytes 393220
  4.5 0.9 %copy-start.4 = (f32[8,32,128]{2,1,0:T(8,128)S(1)}, f32[8,32,128]{2,1,0:T(8,128)}, u32[]{:S(2)}) copy-start(f32[8,32,128]{2,1,0:T(8,128)} %chi_in.1) | copy-start | bytes 393220
  5.4 0.8 %copy-start.5 = (s32[2,32,128]{2,1,0:T(8,128)S(1)}, s32[2,32,128]{2,1,0:T(8,128)}, u32[]{:S(2)}) copy-start(s32[2,32,128]{2,1,0:T(8,128)} %cls_ref.1) | copy-start | bytes 98308
  6.2 0.7 %copy-start.6 = (f32[8]{0:T(128)S(1)}, f32[8]{0:T(128)}, u32[]{:S(2)}) copy-start(f32[8]{0:T(128)} %eps_tab.1) | copy-start | bytes 100
  6.8 0.7 %copy-start.7 = (f32[8]{0:T(128)S(1)}, f32[8]{0:T(128)}, u32[]{:S(2)}) copy-start(f32[8]{0:T(128)} %chi_tab.1) | copy-start | bytes 100

commit v2 on v1

--- a/solution.py
+++ b/solution.py
@@ -18,9 +18,9 @@
 
 def kernel(
     gz_name, gx_name, gz_count, gx_count,
-    d_in, e_in, h_in, eps_in, chi_in, cls_ref, eps_tab, chi_tab,
+    d_in, e_in, h_in, eps_in, chi_in, cls_in, eps_tab_in, chi_tab_in,
     d_out, e_out, h_out, eps_out, chi_out,
-    F, EX, SE, SU, SL, RU, RL, load_sem, send_sem, recv_sem,
+    F, EX, SE, HX, SU, SL, RU, RL, cls_ref, eps_tab, chi_tab, load_sem, send_sem, recv_sem,
 ):
     planes, rows, lanes = d_in.shape[1], d_in.shape[2], d_in.shape[3]
     wide = rows + 2 * HALO
@@ -43,7 +43,11 @@
             ]
         )
     ]
-    for c in loads:
+    extra = [
+        pltpu.make_async_copy(src, dst, load_sem.at[5 + i])
+        for i, (src, dst) in enumerate([(cls_in, cls_ref), (eps_tab_in, eps_tab), (chi_tab_in, chi_tab)])
+    ]
+    for c in loads + extra:
         c.start()
 
     barrier = pltpu.get_barrier_semaphore()
@@ -91,13 +95,9 @@
             pl.when(to)(copy.wait_send)
 
     top = LOW + planes
-    last = pl.ds(planes - LOW, LOW)
     up_main = [
-        remote(e_in.at[:, last], F.at[pl.ds(0, 3), pl.ds(0, LOW), own], 1, 0),
-        remote(h_in.at[:, last], F.at[pl.ds(3, 3), pl.ds(0, LOW), own], 1, 0),
-        remote(d_in.at[:, planes - 1], F.at[pl.ds(6, 3), LOW - 1, own], 1, 0),
-        remote(eps_in.at[planes - 1], F.at[9, LOW - 1, own], 1, 0),
-        remote(chi_in.at[planes - 1], F.at[10, LOW - 1, own], 1, 0),
+        remote(e_in.at[:, planes - 1], F.at[pl.ds(0, 3), LOW - 1, own], 1, 0),
+        remote(h_in.at[pl.ds(0, 2), planes - 1], F.at[pl.ds(3, 2), LOW - 1, own], 1, 0),
     ]
     first = pl.ds(0, ADVANCE)
     above = pl.ds(top, ADVANCE)
@@ -112,13 +112,12 @@
     side, up_diag, dn_diag = [], [], []
     for S, R, dx in ((SU, RU, -1), (SL, RL, 1)):
         side.append(remote(S, R.at[:, every], 0, dx))
-        up_diag.append(remote(S.at[:, planes - 1], R.at[:, LOW - 1], 1, dx))
-        up_diag.append(
-            remote(S.at[pl.ds(0, 5), pl.ds(planes - LOW, LOW - 1)], R.at[pl.ds(0, 5), pl.ds(0, LOW - 1)], 1, dx)
-        )
+        up_diag.append(remote(S.at[pl.ds(0, 5), planes - 1], R.at[pl.ds(0, 5), LOW - 1], 1, dx))
         dn_diag.append(remote(S.at[:, first], R.at[:, above], -1, dx))
         dn_diag.append(remote(S.at[pl.ds(0, 2), ADVANCE], R.at[pl.ds(0, 2), top + ADVANCE], -1, dx))
     e_down = [remote(SE.at[s], EX.at[s + 1], -1, 0) for s in range(STEPS - 1)]
+
+    h_up = [remote(F.at[pl.ds(3, 2), top + ADVANCE - 1], HX, 1, 0)]
 
     start(up_main)
     for c in loads:
@@ -136,6 +135,8 @@
     start(dn_diag)
 
     is_top = jnp.logical_not(has_up)
+    for c in extra:
+        c.wait()
 
     @pl.when(is_top)
     def _():
@@ -193,9 +194,8 @@
         F[5, q] = hz
         return (ex, ey, ez), (hx, hy, hz)
 
-    def plane_update(q, e_above, outside):
-        (ex, ey, ez), (hx, hy, hz) = h_update(q, e_above)
-        bx, by = F[3, q - 1], F[4, q - 1]
+    def de_update(q, e_old, h_new, below, outside):
+        (ex, ey, ez), (hx, hy, hz), (bx, by) = e_old, h_new, below
         dx = F[6, q] + COURANT * ((hz - y_prev(hz)) - (hy - by))
         dy = F[7, q] + COURANT * ((hx - bx) - (hz - x_prev(hz)))
         dz = F[8, q] + COURANT * ((hy - x_prev(hy)) - (hx - y_prev(hx)))
@@ -211,6 +211,10 @@
         F[1, q] = jnp.where(off, 0.0, ey)
         F[2, q] = jnp.where(off, 0.0, ez)
 
+    def plane_update(q, e_above, outside):
+        e_old, h_new = h_update(q, e_above)
+        de_update(q, e_old, h_new, (F[3, q - 1], F[4, q - 1]), outside)
+
     def from_above(q):
         return F[0, q + 1], F[1, q + 1]
 
@@ -227,13 +231,12 @@
     lax.fori_loop(LOW, top, join_own, 0)
     arrive(up_main)
     arrive(up_diag)
-    for q in range(LOW - 1):
-        join(q, 5)
-    join(LOW - 1, 11)
+    join(LOW - 1, 5)
 
     for s in range(1, STEPS + 1):
-        h_update(s - 1, from_above(s - 1))
-        lax.fori_loop(s, top - s, sweep, 0)
+        low = jnp.where(has_dn, LOW - 1 + s, LOW).astype(jnp.int32)
+        h_update(low - 1, from_above(low - 1))
+        lax.fori_loop(low, top - s, sweep, 0)
         if s < STEPS:
             SE[s - 1] = F[0:2, LOW + ADVANCE]
             start(e_down[s - 1 : s])
@@ -252,12 +255,21 @@
                 F[c, top + q] = jnp.zeros((wide, lanes), jnp.float32)
         EX[0] = jnp.zeros((2, wide, lanes), jnp.float32)
 
-    for s in range(1, STEPS + 1):
-        lax.fori_loop(top - s, top + ADVANCE - 1, sweep, 0)
+    edge = top + ADVANCE - 1
+    for s in range(1, STEPS):
+        lax.fori_loop(top - s, edge, sweep, 0)
         if s > 1:
             arrive(e_down[s - 2 : s - 1])
-        q = top + ADVANCE - 1
-        plane_update(q, (EX[s - 1, 0], EX[s - 1, 1]), is_top)
+        plane_update(edge, (EX[s - 1, 0], EX[s - 1, 1]), is_top)
+    arrive(e_down[STEPS - 2 :])
+    h_update(edge, (EX[STEPS - 1, 0], EX[STEPS - 1, 1]))
+    start(h_up)
+    lax.fori_loop(top - STEPS, edge, sweep, 0)
+
+    def held(c, q):
+        return F[c, q], F[c + 1, q], F[c + 2, q]
+
+    de_update(edge, held(0, edge), held(3, edge), (F[3, edge - 1], F[4, edge - 1]), is_top)
 
     @pl.when(is_top)
     def _():
@@ -265,28 +277,51 @@
             for q in range(ADVANCE):
                 F[c, top + q] = jnp.zeros((wide, lanes), jnp.float32)
 
-    moved = pl.ds(LOW + ADVANCE, planes)
+    begin = LOW + ADVANCE
+    moved = pl.ds(begin, planes)
+    rest = pl.ds(begin + 1, planes - 1)
+    later = pl.ds(1, planes - 1)
     stores = [
-        pltpu.make_async_copy(F.at[at, moved, own], dst, load_sem.at[i])
-        for i, (dst, at) in enumerate(
+        pltpu.make_async_copy(src, dst, load_sem.at[i])
+        for i, (src, dst) in enumerate(
             [
-                (e_out, pl.ds(0, 3)),
-                (h_out, pl.ds(3, 3)),
-                (d_out, pl.ds(6, 3)),
-                (eps_out, 9),
-                (chi_out, 10),
+                (F.at[pl.ds(3, 3), moved, own], h_out),
+                (F.at[9, moved, own], eps_out),
+                (F.at[10, moved, own], chi_out),
+                (F.at[pl.ds(0, 3), rest, own], e_out.at[:, later]),
+                (F.at[pl.ds(6, 3), rest, own], d_out.at[:, later]),
+                (F.at[pl.ds(0, 3), begin, own], e_out.at[:, 0]),
+                (F.at[pl.ds(6, 3), begin, own], d_out.at[:, 0]),
             ]
         )
     ]
-    for c in stores:
+    for c in stores[:5]:
         c.start()
-    for group in (up_main, side, up_diag, dn_main, dn_diag, e_down):
+    arrive(h_up)
+
+    @pl.when(has_dn)
+    def _():
+        de_update(begin, held(0, begin), held(3, begin), (HX[0], HX[1]), False)
+
+    for c in stores[5:]:
+        c.start()
+    for group in (up_main, side, up_diag, dn_main, dn_diag, e_down, h_up):
         sent(group)
     for c in stores:
         c.wait()
 
 
-N_COPIES = 5 + 6 + 10 + STEPS - 1
+def copy_kernel(*refs):
+    count = len(refs) // 2
+    sem = refs[-1]
+    copies = [pltpu.make_async_copy(refs[i], refs[count + i], sem.at[i]) for i in range(count)]
+    for c in copies:
+        c.start()
+    for c in copies:
+        c.wait()
+
+
+N_COPIES = 2 + 6 + 8 + STEPS - 1 + 1
 
 
 def on_device(mesh, d_field, e_field, h_field, permittivity, kerr_coeff, classes, eps_table, chi_table):
@@ -295,31 +330,42 @@
     wide = rows + 2 * HALO
     depth = LOW + planes + ADVANCE
     f32 = jnp.float32
-    hbm = pl.BlockSpec(memory_space=pl.ANY)
-    smem = pl.BlockSpec(memory_space=pltpu.SMEM)
-    vmem = pl.BlockSpec(memory_space=pltpu.VMEM)
-    return pl.pallas_call(
+    hbm = pl.BlockSpec(memory_space=pltpu.HBM)
+    results = pl.pallas_call(
         functools.partial(kernel, gz_name, gx_name, mesh.shape[gz_name], mesh.shape[gx_name]),
         out_shape=[jax.ShapeDtypeStruct(a.shape, f32) for a in (d_field, e_field, h_field, permittivity, kerr_coeff)],
-        in_specs=[hbm] * 5 + [vmem, smem, smem],
+        in_specs=[hbm] * 8,
         out_specs=[hbm] * 5,
         scratch_shapes=[
             pltpu.VMEM((11, depth, wide, lanes), f32),
             pltpu.VMEM((STEPS, 2, wide, lanes), f32),
             pltpu.VMEM((STEPS - 1, 2, wide, lanes), f32),
+            pltpu.VMEM((2, wide, lanes), f32),
             pltpu.VMEM((11, planes, HALO, lanes), f32),
             pltpu.VMEM((11, planes, HALO, lanes), f32),
             pltpu.VMEM((11, depth + 1, HALO, lanes), f32),
             pltpu.VMEM((11, depth + 1, HALO, lanes), f32),
-            pltpu.SemaphoreType.DMA((5,)),
+            pltpu.VMEM(classes.shape, jnp.int32),
+            pltpu.SMEM(eps_table.shape, f32),
+            pltpu.SMEM(chi_table.shape, f32),
+            pltpu.SemaphoreType.DMA((8,)),
             pltpu.SemaphoreType.DMA((N_COPIES,)),
             pltpu.SemaphoreType.DMA((N_COPIES,)),
         ],
         compiler_params=pltpu.CompilerParams(
-            collective_id=0, has_side_effects=True, vmem_limit_bytes=32 * 1024 * 1024
+            collective_id=0, has_side_effects=True, vmem_limit_bytes=60 * 1024 * 1024
         ),
         name="window",
     )(d_field, e_field, h_field, permittivity, kerr_coeff, classes, eps_table, chi_table)
+    return pl.pallas_call(
+        copy_kernel,
+        out_shape=[jax.ShapeDtypeStruct(r.shape, f32) for r in results],
+        in_specs=[hbm] * 5,
+        out_specs=[hbm] * 5,
+        scratch_shapes=[pltpu.SemaphoreType.DMA((5,))],
+        compiler_params=pltpu.CompilerParams(vmem_limit_bytes=60 * 1024 * 1024),
+        name="place",
+    )(*results)
 
 
 def solution(mesh):

time: 44.7 us -> 74.9 us (1.68)
  Pallas kernels: 33.3 us -> 74.1 us
  local copies, waits for them, and re-layouts: 10.4 us -> 0 us
    pallas_call x0 -> x1, Pallas kernels: none -> 44.8 us  [on_device(): pl.pallas_call(copy_kernel, out_shape=[jax.ShapeDtypeStruct(r.shape, f32)...]
    unnamed x21 -> x0, local copies, waits for them, and re-layouts: 10.4 us -> none
    pallas_call x1, Pallas kernels: 33.3 us -> 29.3 us  [on_device(): pl.pallas_call(functools.partial(kernel, gz_name, gx_name, mesh.shape[gz_...]
where the time goes in v2:
time: 74.9 us; the launch traced here: 74.7 us
  Pallas kernels  74.1 us (99%)
    pallas_call x1, Pallas kernels, on_device(): pl.pallas_call(copy_kernel, out_shape=[jax.ShapeDtypeStruct(r.shape, f32)...  44.8 us
    pallas_call x1, Pallas kernels, on_device(): pl.pallas_call(functools.partial(kernel, gz_name, gx_name, mesh.shape[gz_...  29.3 us

profile of v2, /device:TPU:0, one launch (start us, length us, event | category | flops | bytes accessed | tf_op | source)
XLA Modules:
  0.0 74.7 jit_solution(12017724223567756838)
XLA Ops:
  0.6 29.3 %window.1 = (f32[3,8,32,128]{3,2,1,0:T(8,128)}, f32[3,8,32,128]{3,2,1,0:T(8,128)}, f32[3,8,32,128]{3,2,1,0:T(8,128)}, f32[8,32,128]{2,1,0:T(8,128)}, f32[8,32,128]{2,1,0:T(8,128)}) custom-call(f32[3,8,32,128]{3,2,1,0:T(8,128)} %d_in.1, f32[3,8,32,128]{3,2,1,0:T(8,128)} %e_in.1, f32[3,8,32,128]{3,2,1,0:T(8,128)} %h_in.1, f32[8,32,128]{2,1,0:T(8,128)} %eps_in.1, ...), custom_call_target="tpu_custom_call" | custom-call | tf_op jit(solution)/shard_map/window/pallas_call | solution.py:334
  29.9 44.8 %place.1 = (f32[3,8,32,128]{3,2,1,0:T(8,128)}, f32[3,8,32,128]{3,2,1,0:T(8,128)}, f32[3,8,32,128]{3,2,1,0:T(8,128)}, f32[8,32,128]{2,1,0:T(8,128)}, f32[8,32,128]{2,1,0:T(8,128)}) custom-call(f32[3,8,32,128]{3,2,1,0:T(8,128)} %get-tuple-element.10.refs_0_, f32[3,8,32,128]{3,2,1,0:T(8,128)} %get-tuple-element.11.refs_1_, ...), custom_call_target="tpu_custom_call" | custom-call | tf_op jit(solution)/shard_map/place/pallas_call | solution.py:360
